TPU v7x, 32 devices: a whole 2x2x4 slice. The times are simulated.
32 devices in a mesh: dp: 16 (over z, x, core), tp: 2 (over y).
Axes of the slice: x: 2, y: 2, z: 4, core: 2. Of those that a mesh axis runs over, the one named last changes fastest.
Arguments:
- tokens: bfloat16 [8192, 1152], P('dp'), may hold values from -6 to 6
- condition: float32 [32, 1152], P('dp'), may hold values from -6 to 6
- noise_times: float32 [32], P('dp'), may hold values from 0 to 1
- cotangent: bfloat16 [8192, 1152], P('dp'), may hold values from -6 to 6
- ada_weight: bfloat16 [1152, 6912], P(None, 'tp'), may hold values from -0.1875 to 0.1875
- ada_bias: float32 [6912], P('tp'), may hold values from -3 to 3
- qkv_weight: bfloat16 [1152, 3, 1152], P(None, None, 'tp'), may hold values from -0.1875 to 0.1875
- qv_bias: float32 [2, 1152], P(None, 'tp'), may hold values from -3 to 3
- out_weight: bfloat16 [1152, 1152], P('tp'), may hold values from -1.5 to 1.5
- out_bias: float32 [1152], replicated, may hold values from -3 to 3
- fc1_weight: bfloat16 [1152, 4608], P(None, 'tp'), may hold values from -0.1875 to 0.1875
- fc1_bias: float32 [4608], P('tp'), may hold values from -3 to 3
- fc2_weight: bfloat16 [4608, 1152], P('tp'), may hold values from -0.09375 to 0.09375
- fc2_bias: float32 [1152], replicated, may hold values from -3 to 3
Outputs:
- output: bfloat16 [8192, 1152], P('dp')
- grad_tokens: bfloat16 [8192, 1152], P('dp')
- grad_condition: float32 [32, 1152], P('dp')
- grad_ada_weight: float32 [1152, 6912], P('dp', 'tp')
- grad_ada_bias: float32 [6912], P('tp')
- grad_qkv_weight: float32 [1152, 3, 1152], P('dp', None, 'tp')
- grad_qv_bias: float32 [2, 1152], P(None, 'tp')
- grad_out_weight: float32 [1152, 1152], P('tp', 'dp')
- grad_out_bias: float32 [1152], replicated
- grad_fc1_weight: float32 [1152, 4608], P('dp', 'tp')
- grad_fc1_bias: float32 [4608], P('tp')
- grad_fc2_weight: float32 [4608, 1152], P('tp', 'dp')
- grad_fc2_bias: float32 [1152], replicated
All inputs are finite; a program needn't handle non-finite values.
Results may differ from a plain program's by a relative error of at most 0.02.
The roundings to bfloat16 on the way count: a program that leaves them out, or rounds other values in their place, can miss the bound.
Values may be sent and summed in bfloat16 or wider, within the bound.
A program may use at most 192 MiB of HBM per device.

v0:
```python
import math

import jax
import jax.numpy as jnp
from jax import lax
from jax.sharding import PartitionSpec as P

D = 1152
HEAD_DIM = 72
SEQ = 256


norm_eps = 1e-06
gelu_coef = 0.7978845608028654


def layer_norm(values):
    center = values - jnp.mean(values, axis=-1, keepdims=True)
    variance = jnp.mean(center * center, axis=-1, keepdims=True)
    return center * lax.rsqrt(variance + norm_eps)


def gelu_tanh(values):
    return (
        0.5 * values * (1.0 + jnp.tanh(gelu_coef * (values + 0.044715 * values * values * values)))
    )


def time_features(noise_times):
    half_width = D // 2
    ladder = jnp.arange(half_width).astype(jnp.float32)
    frequency = jnp.exp(-math.log(10000.0) * ladder / half_width)
    angles = 1000.0 * noise_times[:, None] * frequency[None, :]
    return jnp.concatenate([jnp.cos(angles), jnp.sin(angles)], axis=1)


def contract_rows(former, latter):
    return lax.dot_general(
        former, latter, (((0,), (0,)), ((), ())), preferred_element_type=jnp.float32
    )


def contract_cols(former, latter):
    return lax.dot_general(
        former, latter, (((1,), (1,)), ((), ())), preferred_element_type=jnp.float32
    )


def feed_up(input_b, fc1_weight, fc1_bias, fc2_weight):
    hidden_pre = jnp.dot(input_b, fc1_weight, preferred_element_type=jnp.float32) + fc1_bias
    hidden_act, gelu_pull = jax.vjp(gelu_tanh, hidden_pre)
    hidden = hidden_act.astype(jnp.bfloat16)
    return (hidden, gelu_pull, jnp.dot(hidden, fc2_weight, preferred_element_type=jnp.float32))


def local(
    tokens,
    condition,
    noise_times,
    cotangent,
    ada_weight,
    ada_bias,
    qkv_weight,
    qv_bias,
    out_weight,
    out_bias,
    fc1_weight,
    fc1_bias,
    fc2_weight,
    fc2_bias,
):
    images = condition.shape[0]
    row_count = tokens.shape[0]
    local_width = qkv_weight.shape[2]
    local_heads = local_width // HEAD_DIM
    ada_cols = ada_weight.shape[1]
    score_scale = 1.0 / math.sqrt(HEAD_DIM)
    cond_total = condition + time_features(noise_times)
    silu_cond, silu_pull = jax.vjp(jax.nn.silu, cond_total)
    silu_low = silu_cond.astype(jnp.bfloat16)
    mod_part = jnp.dot(silu_low, ada_weight, preferred_element_type=jnp.float32) + ada_bias
    modulation = lax.all_gather(mod_part, "tp", axis=1, tiled=True)
    pieces = modulation.reshape(images, 6, 1, D)
    residual = tokens.astype(jnp.float32).reshape(images, SEQ, D)
    normed_one, norm_one_pull = jax.vjp(layer_norm, residual)
    input_a = (
        (normed_one * (1.0 + pieces[:, 1]) + pieces[:, 0])
        .astype(jnp.bfloat16)
        .reshape(row_count, D)
    )
    qkv_flat = qkv_weight.reshape(D, 3 * local_width)
    projected = jnp.dot(input_a, qkv_flat, preferred_element_type=jnp.float32).reshape(
        images, SEQ, 3, local_heads, HEAD_DIM
    )
    queries = (projected[:, :, 0] + qv_bias[0].reshape(local_heads, HEAD_DIM)).astype(jnp.bfloat16)
    key_rows = projected[:, :, 1].astype(jnp.bfloat16)
    value_rows = (projected[:, :, 2] + qv_bias[1].reshape(local_heads, HEAD_DIM)).astype(
        jnp.bfloat16
    )
    scores = (
        jnp.einsum("nqhd,nkhd->nhqk", queries, key_rows, preferred_element_type=jnp.float32)
        * score_scale
    )
    log_total = jax.nn.logsumexp(scores, axis=-1, keepdims=True)
    weights = jnp.exp(scores - log_total)
    weights_low = weights.astype(jnp.bfloat16)
    attended = (
        jnp.einsum("nhqk,nkhd->nqhd", weights_low, value_rows, preferred_element_type=jnp.float32)
        .astype(jnp.bfloat16)
        .reshape(row_count, local_width)
    )
    attn_part = jnp.dot(attended, out_weight, preferred_element_type=jnp.float32)
    attention = lax.psum(attn_part, "tp") + out_bias
    attention = attention.reshape(images, SEQ, D)
    middle = residual + pieces[:, 2] * attention
    normed_two, norm_two_pull = jax.vjp(layer_norm, middle)
    input_b = (
        (normed_two * (1.0 + pieces[:, 4]) + pieces[:, 3])
        .astype(jnp.bfloat16)
        .reshape(row_count, D)
    )
    hidden, gelu_pull, mlp_part = feed_up(input_b, fc1_weight, fc1_bias, fc2_weight)
    branch = lax.psum(mlp_part.astype(jnp.bfloat16), "tp").astype(jnp.float32) + fc2_bias
    branch = branch.reshape(images, SEQ, D)
    output = (middle + pieces[:, 5] * branch).reshape(row_count, D).astype(jnp.bfloat16)
    grad_out = cotangent.astype(jnp.float32).reshape(images, SEQ, D)
    grad_gate_two = jnp.sum(grad_out * branch, axis=1)
    grad_branch = (grad_out * pieces[:, 5]).astype(jnp.bfloat16).reshape(row_count, D)
    bias_fc2 = jnp.sum(grad_branch.astype(jnp.float32), axis=0)
    weight_fc2 = contract_rows(hidden, grad_branch)
    grad_hidden = contract_cols(grad_branch, fc2_weight)
    grad_pre = gelu_pull(grad_hidden)[0].astype(jnp.bfloat16)
    bias_fc1 = jnp.sum(grad_pre.astype(jnp.float32), axis=0)
    weight_fc1 = contract_rows(input_b, grad_pre)
    grad_input_b = lax.psum(contract_cols(grad_pre, fc1_weight), "tp").reshape(images, SEQ, D)
    grad_shift_two = jnp.sum(grad_input_b, axis=1)
    grad_scale_two = jnp.sum(grad_input_b * normed_two, axis=1)
    grad_middle = grad_out + norm_two_pull(grad_input_b * (1.0 + pieces[:, 4]))[0]
    grad_gate_one = jnp.sum(grad_middle * attention, axis=1)
    grad_attention = (grad_middle * pieces[:, 2]).astype(jnp.bfloat16).reshape(row_count, D)
    bias_out = jnp.sum(grad_attention.astype(jnp.float32), axis=0)
    weight_out = contract_rows(attended, grad_attention)
    grad_attended = (
        contract_cols(grad_attention, out_weight)
        .astype(jnp.bfloat16)
        .reshape(images, SEQ, local_heads, HEAD_DIM)
    )
    scores_again = (
        jnp.einsum("nqhd,nkhd->nhqk", queries, key_rows, preferred_element_type=jnp.float32)
        * score_scale
    )
    soft_rows = jnp.exp(scores_again - log_total)
    soft_low = soft_rows.astype(jnp.bfloat16)
    grad_values = jnp.einsum(
        "nhqk,nqhd->nkhd", soft_low, grad_attended, preferred_element_type=jnp.float32
    ).astype(jnp.bfloat16)
    grad_soft = jnp.einsum(
        "nqhd,nkhd->nhqk", grad_attended, value_rows, preferred_element_type=jnp.float32
    )
    row_dot = jnp.sum(soft_rows * grad_soft, axis=-1, keepdims=True)
    grad_scores = (soft_rows * (grad_soft - row_dot)).astype(jnp.bfloat16)
    grad_queries = (
        jnp.einsum("nhqk,nkhd->nqhd", grad_scores, key_rows, preferred_element_type=jnp.float32)
        * score_scale
    ).astype(jnp.bfloat16)
    grad_keys = (
        jnp.einsum("nhqk,nqhd->nkhd", grad_scores, queries, preferred_element_type=jnp.float32)
        * score_scale
    ).astype(jnp.bfloat16)
    grad_projected = jnp.stack([grad_queries, grad_keys, grad_values], axis=2).reshape(
        row_count, 3 * local_width
    )
    bias_qv = jnp.stack(
        [
            jnp.sum(grad_queries.astype(jnp.float32), axis=(0, 1)).reshape(local_width),
            jnp.sum(grad_values.astype(jnp.float32), axis=(0, 1)).reshape(local_width),
        ]
    )
    weight_qkv = contract_rows(input_a, grad_projected).reshape(D, 3, local_width)
    grad_input_a = lax.psum(contract_cols(grad_projected, qkv_flat), "tp").reshape(images, SEQ, D)
    grad_shift_one = jnp.sum(grad_input_a, axis=1)
    grad_scale_one = jnp.sum(grad_input_a * normed_one, axis=1)
    grad_tokens = (
        (grad_middle + norm_one_pull(grad_input_a * (1.0 + pieces[:, 1]))[0])
        .reshape(row_count, D)
        .astype(jnp.bfloat16)
    )
    grad_mod = jnp.stack(
        [
            grad_shift_one,
            grad_scale_one,
            grad_gate_one,
            grad_shift_two,
            grad_scale_two,
            grad_gate_two,
        ],
        axis=1,
    ).reshape(images, 6 * D)
    grad_mod_mine = lax.dynamic_slice_in_dim(grad_mod, lax.axis_index("tp") * ada_cols, ada_cols, 1)
    bias_ada = jnp.sum(grad_mod_mine, axis=0)
    weight_ada = lax.dot_general(
        silu_low.astype(jnp.float32),
        grad_mod_mine,
        (((0,), (0,)), ((), ())),
        precision=lax.Precision.HIGHEST,
        preferred_element_type=jnp.float32,
    )
    silu_part = lax.dot_general(
        grad_mod_mine,
        ada_weight.astype(jnp.float32),
        (((1,), (1,)), ((), ())),
        precision=lax.Precision.HIGHEST,
        preferred_element_type=jnp.float32,
    )
    grad_silu = lax.psum(silu_part, "tp")
    grad_condition = silu_pull(grad_silu)[0]
    factor = 1.0 / math.sqrt(row_count * lax.axis_size("dp"))
    sum_ada, sum_qkv, sum_out, sum_fc1, sum_fc2 = (
        lax.psum_scatter(
            weight_ada.astype(jnp.bfloat16), "dp", scatter_dimension=0, tiled=True
        ).astype(jnp.float32),
        lax.psum_scatter(
            weight_qkv.astype(jnp.bfloat16), "dp", scatter_dimension=0, tiled=True
        ).astype(jnp.float32),
        lax.psum_scatter(
            weight_out.astype(jnp.bfloat16), "dp", scatter_dimension=1, tiled=True
        ).astype(jnp.float32),
        lax.psum_scatter(
            weight_fc1.astype(jnp.bfloat16), "dp", scatter_dimension=0, tiled=True
        ).astype(jnp.float32),
        lax.psum_scatter(
            weight_fc2.astype(jnp.bfloat16), "dp", scatter_dimension=1, tiled=True
        ).astype(jnp.float32),
    )
    total_ada, total_qv, total_out, total_fc1, total_fc2 = lax.psum(
        (bias_ada, bias_qv, bias_out, bias_fc1, bias_fc2), "dp"
    )
    return (
        output,
        grad_tokens,
        grad_condition,
        sum_ada * factor,
        total_ada * factor,
        sum_qkv * factor,
        total_qv * factor,
        sum_out * factor,
        total_out * factor,
        sum_fc1 * factor,
        total_fc1 * factor,
        sum_fc2 * factor,
        total_fc2 * factor,
    )


def solution(mesh):
    return jax.shard_map(
        local,
        mesh=mesh,
        in_specs=(
            P("dp", None),
            P("dp", None),
            P("dp"),
            P("dp", None),
            P(None, "tp"),
            P("tp"),
            P(None, None, "tp"),
            P(None, "tp"),
            P("tp", None),
            P(),
            P(None, "tp"),
            P("tp"),
            P("tp", None),
            P(),
        ),
        out_specs=(
            P("dp", None),
            P("dp", None),
            P("dp", None),
            P("dp", "tp"),
            P("tp"),
            P("dp", None, "tp"),
            P(None, "tp"),
            P("tp", "dp"),
            P(),
            P("dp", "tp"),
            P("tp"),
            P("tp", "dp"),
            P(),
        ),
        check_vma=False,
    )
```

profile of v0, /device:TPU:0, one launch (start us, length us, event | category | flops | bytes accessed | tf_op | source)
XLA Modules:
  0.0 755.9 jit_solution(10860789326381250144)
XLA Ops:
  7.3 0.7 broadcast_multiply_fusion.7
  8.0 1.5 convert_reduce_fusion.3
  9.5 1.7 multiply_reduce_fusion.6
  11.6 4.5 convolution_add_fusion.1
  16.2 5.5 all_gather.3
  21.8 0.7 fusion.14
  22.5 5.1 fusion.62
  27.6 0.9 multiply_reduce_fusion.1
  28.5 0.7 exponential_reduce_fusion
  29.4 0.9 fusion.25
  31.4 2.6 fusion.63
  34.3 2.6 convert_reduce_fusion.1
  36.9 67.7 %all-reduce.8.cloned.1.call-done = f32[512,1152]{1,0:T(8,128)} async-done(((f32[512,1152]{1,0:T(8,128)}), f32[512,1152]{1,0:T(8,128)}) %all-reduce.8.cloned.1.call-update) | async-done | bytes 2359312 | tf_op jit(solution)/shard_map/psum | solution.py:113
  104.7 2.1 fusion.60
  107.2 1.1 copy-done.5
  109.0 6.6 convolution_add_fusion
  115.6 6.8 convert_reduce_fusion
  122.4 1.4 copy-done.29
  123.8 4.7 fusion.64
  128.6 9.0 %convolution_convert_fusion.5 = bf16[512,1152]{1,0:T(8,128)(2,1)} fusion(bf16[2304,1152]{1,0:T(8,128)(2,1)} %param.26, f32[512,2304]{1,0:T(8,128)} %copy-done.28), kind=kOutput, calls=%fused_computation.35 | convolution fusion | flops 2729115648 | bytes 11206656 | tf_op jit(solution)/shard_map/dot_general | solution.py:53
  138.1 59.2 %all-reduce.12.cloned.1.call-done = f32[512,1152]{1,0:T(8,128)} async-done(((f32[512,1152]{1,0:T(8,128)}), f32[512,1152]{1,0:T(8,128)}) %all-reduce.12.cloned.1.call-update) | async-done | bytes 2359312 | tf_op jit(solution)/shard_map/psum | solution.py:135
  197.3 2.8 multiply_reduce_fusion.4
  200.1 43.0 %all-reduce.10.cloned.1.call-done = bf16[512,1152]{1,0:T(8,128)(2,1)} async-done(((bf16[512,1152]{1,0:T(8,128)(2,1)}), bf16[512,1152]{1,0:T(8,128)(2,1)}) %all-reduce.10.cloned.1.call-update) | async-done | bytes 1179664 | tf_op jit(solution)/shard_map/psum | solution.py:123
  243.1 4.8 fusion.59
  248.4 0.9 copy-done.7
  249.4 1.1 copy-done.20
  250.5 1.8 convolution_convert_fusion.7
  252.3 1.9 reshape.280
  254.2 3.4 convert_reduce_fusion.4
  257.7 2.6 multiply_reduce_fusion
  260.3 1.1 multiply_convert_fusion.1
  261.4 0.9 copy-done.12
  262.3 0.8 fusion.24
  263.8 1.8 copy.68
  266.1 1.2 copy-done.13
  267.3 4.0 fusion.65
  271.4 3.6 convolution_convert_fusion.4
  275.3 8.5 %convolution_convert_fusion.1 = bf16[2304,1152]{0,1:T(8,128)(2,1)} fusion(bf16[512,1152]{1,0:T(8,128)(2,1)S(1)} %copy-done.15, f32[512,2304]{1,0:T(8,128)} %copy-done.28), kind=kOutput, calls=%fused_computation.1 | convolution fusion | flops 2731180032 | bytes 11206656 | tf_op jit(solution)/shard_map/dot_general | solution.py:38
  283.9 1.2 copy-done.19
  285.1 6.9 convolution_convert_fusion.2
  292.1 1.2 copy-done.17
  293.3 4.1 convolution_convert_fusion.3
  297.4 18.2 %copy.77 = bf16[1152,3,576]{2,1,0:T(4,128)(2,1)} copy(bf16[1152,3,576]{2,0,1:T(8,128)(2,1)S(1)} %convolution_convert_fusion.3) | data formatting | bytes 7962624
  315.7 12.3 %reshape.292 = bf16[1152,1728]{1,0:T(8,128)(2,1)} reshape(bf16[1152,3,576]{2,1,0:T(4,128)(2,1)} %copy.77) | data formatting | bytes 7962624
  328.3 11.8 %all-reduce.14.cloned.1.call-done = f32[512,1152]{1,0:T(8,128)} async-done(((f32[512,1152]{1,0:T(8,128)}), f32[512,1152]{1,0:T(8,128)}) %all-reduce.14.cloned.1.call-update) | async-done | bytes 2359312 | tf_op jit(solution)/shard_map/psum | solution.py:180
  340.2 5.6 fusion.21
  346.0 8.7 %convolution_convert_fusion = bf16[1152,3456]{1,0:T(8,128)(2,1)} fusion(f32[2,6912]{1,0:T(2,128)S(1)} %bitcast.198, s32[]{:T(128)S(6)} %select_n.15, f32[2,1152]{1,0:T(2,128)S(1)} %copy-done.21, f32[2,576]{1,0:T(2,128)S(1)} %get-tuple-element.46, f32[2,576]{1,0:T(2,128)S(1)} %get-tuple-element.45), kind=kOutput, calls=%fused_computation | convolution fusion | flops 99548928 | bytes 8009732 | tf_op jit(solution)/shard_map/dot_general | solution.py:201
  355.0 47.6 %reduce-scatter.20.cloned.1.call-done = bf16[576,72]{0,1:T(8,128)(2,1)} async-done(((bf16[576,1152]{0,1:T(8,128)(2,1)}), bf16[576,72]{0,1:T(8,128)(2,1)}) %reduce-scatter.20.cloned.1.call-update) | async-done | bytes 82960
  402.6 1.6 convert_multiply_fusion.4
  404.1 2.3 multiply_reduce_fusion.3
  406.5 2.6 fusion.55
  409.1 2.1 add_convert_fusion
  411.2 59.3 %all-reduce.2 = (f32[3456]{0:T(1024)S(1)}, f32[2,576]{1,0:T(2,128)S(1)}, f32[1152]{0:T(1024)S(1)}, f32[2304]{0:T(1024)S(1)}, f32[1152]{0:T(1024)S(1)}) all-reduce(f32[3456]{0:T(1024)S(1)} %dynamic-slice_reduce_fusion, f32[2,576]{1,0:T(2,128)S(1)} %pad_maximum_fusion.1, ...), channel_id=1, replica_groups=mesh['dp'=16,'tp'=2] {'dp'}, use_global_device_ids=true, to_apply=%region_24.25 | all-reduce | flops 9216 | bytes 73728 | tf_op jit(solution)/shard_map/psum | solution.py:235
  470.5 8.8 %fusion.45 = f32[2,1152]{1,0:T(2,128)S(1)} fusion(bf16[1152,3456]{1,0:T(8,128)(2,1)} %param.18, f32[2,6912]{1,0:T(2,128)S(1)} %bitcast.200, s32[]{:T(128)S(6)} %select_n.15), kind=kOutput, calls=%fused_computation.103 | convolution fusion | flops 95551488 | bytes 7999492 | tf_op jit(solution)/shard_map/dot_general | solution.py:208
  479.3 5.1 psum.74
  487.4 0.7 fusion.48
  488.1 1.9 convert_multiply_fusion.1
  489.9 78.2 %reduce-scatter.12.cloned.1.call-done = bf16[72,2304]{1,0:T(8,128)(2,1)} async-done(((bf16[1152,2304]{1,0:T(8,128)(2,1)}), bf16[72,2304]{1,0:T(8,128)(2,1)}) %reduce-scatter.12.cloned.1.call-update) | async-done | bytes 331792 | tf_op jit(solution)/shard_map/reduce_scatter | solution.py:228
  568.1 1.9 convert_multiply_fusion.2
  570.0 73.1 %reduce-scatter.16.cloned.1.call-done = bf16[72,1728]{1,0:T(8,128)(2,1)} async-done(((bf16[1152,1728]{1,0:T(8,128)(2,1)}), bf16[72,1728]{1,0:T(8,128)(2,1)}) %reduce-scatter.16.cloned.1.call-update) | async-done | bytes 248848
  643.1 1.1 reshape.293
  644.3 0.9 convert_multiply_fusion.3
  645.1 101.9 %reduce-scatter.18.cloned.1.call-done = bf16[72,3456]{1,0:T(8,128)(2,1)} async-done(((bf16[1152,3456]{1,0:T(8,128)(2,1)}), bf16[72,3456]{1,0:T(8,128)(2,1)}) %reduce-scatter.18.cloned.1.call-update) | async-done | bytes 497680
  747.1 2.1 convert_multiply_fusion
  (134 shorter events, 9.7 us)
Async XLA Ops:
  7.2 24.3 %copy-start = (bf16[576,1152]{1,0:T(8,128)(2,1)S(1)}, bf16[576,1152]{1,0:T(8,128)(2,1)}, u32[]{:S(2)}) copy-start(bf16[576,1152]{1,0:T(8,128)(2,1)} %param.22) | copy-start | bytes 3981316
  7.2 4.1 copy-start.25
  7.2 4.4 copy-start.21
  7.2 4.4 copy-start.24
  7.2 97.4 %all-reduce.8.cloned.1.call-start = ((), (), s32[]{:S(2)}) async-start(), calls=%async_computation.5 | async-start | bytes 4718592 | tf_op jit(solution)/shard_map/psum | solution.py:113
  11.6 10.1 %copy-start.4 = (bf16[512,1152]{1,0:T(8,128)(2,1)S(1)}, bf16[512,1152]{1,0:T(8,128)(2,1)}, u32[]{:S(2)}) copy-start(bf16[512,1152]{1,0:T(8,128)(2,1)} %param.14) | copy-start | bytes 3538948
  22.5 5.1 copy-start.16
  27.6 1.7 copy-start.11
  28.5 2.2 copy-start.2
  34.1 70.6 %copy-start.22 = (f32[1152]{0:T(1024)S(1)}, f32[1152]{0:T(1024)}, u32[]{:S(2)}) copy-start(f32[1152]{0:T(1024)} %param.23) | copy-start | bytes 13828
  34.1 163.2 %all-reduce.12.cloned.1.call-start = ((), (), s32[]{:S(2)}) async-start(), calls=%async_computation.7 | async-start | bytes 4718592 | tf_op jit(solution)/shard_map/psum | solution.py:135
  106.8 1.5 copy-start.5
  107.2 1.7 copy-start.27
  108.3 7.3 slice-start.2
  108.9 6.6 copy-start.18
  108.9 6.6 copy-start.14
  108.9 6.6 slice-start.3
  109.0 14.9 %slice-start = ((s8[5308416]{0:T(1024)(128)(4,1)}), s8[4194304]{0:T(1024)(128)(4,1)S(1)}, s32[]{:S(2)}) async-start(s8[5308416]{0:T(1024)(128)(4,1)} %bitcast.207), calls=%async_computation.14 | async-start | bytes 8388608
  115.5 6.9 copy-start.28
  115.6 8.2 %slice-start.1 = ((s8[5308416]{0:T(1024)(128)(4,1)}), s8[1114112]{0:T(1024)(128)(4,1)S(1)}, s32[]{:S(2)}) async-start(s8[5308416]{0:T(1024)(128)(4,1)} %bitcast.207), calls=%async_computation.15 | async-start | bytes 2228224
  122.4 1.4 copy-start.29
  128.5 114.6 %all-reduce.10.cloned.1.call-start = ((), (), s32[]{:S(2)}) async-start(), calls=%async_computation.6 | async-start | bytes 2359296 | tf_op jit(solution)/shard_map/psum | solution.py:123
  137.6 105.5 %copy-start.23 = (f32[1152]{0:T(1024)S(1)}, f32[1152]{0:T(1024)}, u32[]{:S(2)}) copy-start(f32[1152]{0:T(1024)} %param.27) | copy-start | bytes 13828
  137.6 202.6 %all-reduce.14.cloned.1.call-start = ((), (), s32[]{:S(2)}) async-start(), calls=%async_computation.8 | async-start | bytes 4718592 | tf_op jit(solution)/shard_map/psum | solution.py:180
  243.1 4.8 copy-start.9
  247.9 1.5 copy-start.7
  249.4 1.1 copy-start.20
  254.2 3.5 copy-start.3
  260.3 2.0 copy-start.12
  263.8 3.5 copy-start.26
  266.1 1.2 copy-start.13
  271.4 4.0 copy-start.15
  271.4 131.2 %reduce-scatter.20.cloned.1.call-start = ((), (), s32[]{:S(2)}) async-start(), calls=%async_computation.13 | async-start | bytes 1566720
  275.1 213.0 %reduce-scatter.14.cloned.1.call-start = ((), (), s32[]{:S(2)}) async-start(), calls=%async_computation.10 | async-start | bytes 5640192 | tf_op jit(solution)/shard_map/reduce_scatter | solution.py:231
  283.8 1.3 copy-start.19
  283.8 284.3 %reduce-scatter.12.cloned.1.call-start = ((), (), s32[]{:S(2)}) async-start(), calls=%async_computation.9 | async-start | bytes 5640192 | tf_op jit(solution)/shard_map/reduce_scatter | solution.py:228
  292.0 1.3 copy-start.17
  292.0 351.1 %reduce-scatter.16.cloned.1.call-start = ((), (), s32[]{:S(2)}) async-start(), calls=%async_computation.11 | async-start | bytes 4386816
  328.0 12.2 %copy-start.10 = (bf16[512,1152]{1,0:T(8,128)(2,1)S(1)}, bf16[512,1152]{1,0:T(8,128)(2,1)}, u32[]{:S(2)}) copy-start(bf16[512,1152]{1,0:T(8,128)(2,1)} %param.17) | copy-start | bytes 3538948
  328.0 419.1 %reduce-scatter.18.cloned.1.call-start = ((), (), s32[]{:S(2)}) async-start(), calls=%async_computation.12 | async-start | bytes 8460288
  404.1 4.9 copy-start.8
  406.5 2.6 copy-start.6
  487.4 261.8 %copy-start.1 = (bf16[576,1152]{1,0:T(8,128)(2,1)S(1)}, bf16[576,1152]{1,0:T(8,128)(2,1)}, u32[]{:S(2)}) copy-start(bf16[576,1152]{1,0:T(8,128)(2,1)} %param.22) | copy-start | bytes 3981316
Sparse Core Ops, SparseCore 0:
  34.2 70.4 all-reduce.7
  128.6 68.6 all-reduce.11
  200.2 42.8 all-reduce.9
  271.5 68.6 all-reduce.13
  343.8 58.7 reduce-scatter.19
  406.5 79.2 reduce-scatter.13
  489.7 78.3 reduce-scatter.11
  572.1 71.0 reduce-scatter.15
  647.2 99.8 reduce-scatter.17
where the time goes:
time: 764 us; the launch traced here: 756 us
  waiting for transfers between devices  483 us (63%)
  matrix products  94.9 us (12%)
  blocking collectives  69.8 us (9%)
  local copies, waits for them, and re-layouts  47 us (6%)
  other arithmetic  45.4 us (6%)
  between operations  14.7 us (2%)
    unnamed x12, waiting for transfers between devices  223 us
    reduce_scatter x1, waiting for transfers between devices, local(): lax.psum_scatter(weight_fc1.astype(jnp.bfloat16), 'dp', scatter_dimension...  78.2 us
    psum x1, waiting for transfers between devices, local(): attention = lax.psum(attn_part, 'tp') + out_bias  67.7 us
    psum x1, blocking collectives, local(): lax.psum((bias_ada, bias_qv, bias_out, bias_fc1, bias_fc2), 'dp')  59.3 us
    psum x1, waiting for transfers between devices, local(): lax.psum(contract_cols(grad_pre, fc1_weight), 'tp').reshape(images, SEQ, D)  59.2 us
    psum x1, waiting for transfers between devices, local(): lax.psum(mlp_part.astype(jnp.bfloat16), 'tp').astype(jnp.float32) + fc2_bias  43 us
    unnamed x78, local copies, waits for them, and re-layouts  42 us
    dot_general x4, matrix products, contract_rows(): lax.dot_general(former, latter, (((0,), (0,)), ((), ())), preferred_eleme...  23.2 us
  transfers between devices with their start and end apart: 9, of which 8 were waited for; matrix products, arithmetic and copies ran while one was open for 15% of the time, Pallas kernels for 0%

commit v1 on v0

--- a/solution.py
+++ b/solution.py
@@ -1,8 +1,11 @@
+import functools
 import math
 
 import jax
 import jax.numpy as jnp
 from jax import lax
+from jax.experimental import pallas as pl
+from jax.experimental.pallas import tpu as pltpu
 from jax.sharding import PartitionSpec as P
 
 D = 1152
@@ -53,7 +56,7 @@
     return (hidden, gelu_pull, jnp.dot(hidden, fc2_weight, preferred_element_type=jnp.float32))
 
 
-def local(
+def plain(
     tokens,
     condition,
     noise_times,
@@ -250,6 +253,726 @@
         sum_fc2 * factor,
         total_fc2 * factor,
     )
+
+
+NORM_EPS = 1e-06
+GELU_COEF = 0.7978845608028654
+GELU_CUBE = 0.044715
+MESH = pl.DeviceIdType.MESH
+F32 = jnp.float32
+BF16 = jnp.bfloat16
+
+
+def dot_nn(a, b):
+    return lax.dot_general(a, b, (((1,), (0,)), ((), ())), preferred_element_type=F32)
+
+
+def dot_nt(a, b):
+    return lax.dot_general(a, b, (((1,), (1,)), ((), ())), preferred_element_type=F32)
+
+
+def dot_tn(a, b):
+    return lax.dot_general(a, b, (((0,), (0,)), ((), ())), preferred_element_type=F32)
+
+
+def norm_parts(values):
+    center = values - jnp.mean(values, axis=-1, keepdims=True)
+    scale = lax.rsqrt(jnp.mean(center * center, axis=-1, keepdims=True) + NORM_EPS)
+    return center * scale, scale
+
+
+def fold_rows(values):
+    rows, cols = values.shape
+    return jnp.sum(values.reshape(rows // 8, 8, cols), axis=0)
+
+
+def al(index, unit):
+    return pl.multiple_of(index, unit)
+
+
+RC = 16
+PW = 384
+NP = 3
+
+
+def block_kernel(
+    factor,
+    tok_h, cot_h, ada_h, w3_h, wo_h, w1_h, w2_h, silu_r, adab_r, qvb_r, ob_r, b1_r, b2_r,
+    out_h, gt_h, g2_h, g1_h, g3_h, gmod_o, bfc1_o, brow_o, bqv_o,
+    big, w3, wo, w1, w2, tok, cot, ia, ib, gb, qkv, prob, att, attn, mid, hid, gpre,
+    gibs, gibr, g4, at1, rx, rx3, rz, rz3, ry, ry3, fin, fin3, modb, gmod,
+    ld_sem, out_sem, ss, rs, cred,
+):
+    dp, tp = lax.axis_index("dp"), lax.axis_index("tp")
+    z, x, c = dp // 4, (dp // 2) % 2, dp % 2
+    zp, zh = z % 2, z // 2
+    dev_y = (dp, 1 - tp)
+    dev_c = (z * 4 + x * 2 + 1 - c, tp)
+    dev_x = (z * 4 + (1 - x) * 2 + c, tp)
+    dev_z = ((z + 1 - 2 * zp) * 4 + x * 2 + c, tp)
+    dev_w = (((z + 2) % 4) * 4 + x * 2 + c, tp)
+
+    T, D = tok.shape
+    SEQ = T // 2
+    L = wo_h.shape[0]
+    LP = qkv.shape[2]
+    F = w1.shape[1]
+    A = modb.shape[2]
+    scale = 1.0 / math.sqrt(72)
+    blk = D // 8
+
+    barrier = pltpu.get_barrier_semaphore()
+    for dev in (dev_y, dev_c, dev_x, dev_z, dev_w):
+        pl.semaphore_signal(barrier, inc=1, device_id=dev, device_id_type=MESH)
+
+    counter = [0]
+
+    def remote(src, dst, dev):
+        k = counter[0]
+        counter[0] += 1
+        return pltpu.make_async_remote_copy(
+            src_ref=src, dst_ref=dst, send_sem=ss.at[k], recv_sem=rs.at[k],
+            device_id=dev, device_id_type=MESH,
+        )
+
+    lcount = [0]
+
+    def load(src, dst):
+        k = lcount[0]
+        lcount[0] += 1
+        cp = pltpu.make_async_copy(src, dst, ld_sem.at[k])
+        cp.start()
+        return cp
+
+    ocount = [0]
+
+    def store(src, dst):
+        k = ocount[0]
+        ocount[0] += 1
+        cp = pltpu.make_async_copy(src, dst, out_sem.at[k])
+        cp.start()
+        return cp
+
+    NA = A // PW
+    ld_ada = [load(ada_h.at[:, PW * k : PW * (k + 1)], big.at[k]) for k in range(NA)]
+    ld_tok = load(tok_h, tok)
+    ld_w3 = [load(w3_h.at[j], w3.at[j, 0:L]) for j in range(3)]
+    for j in range(3):
+        w3[j, L:LP, :] = jnp.zeros((LP - L, D), BF16)
+    for j in range(2):
+        wo[j, L:LP, :] = jnp.zeros((LP - L, D), BF16)
+
+    silu = silu_r[...].astype(BF16)
+    for k in range(NA):
+        ld_ada[k].wait()
+        part = dot_nn(silu, big[k])[0:2] + adab_r[:, PW * k : PW * (k + 1)]
+        modb[tp, :, PW * k : PW * (k + 1)] = part
+    pl.semaphore_wait(barrier, 5)
+    pl.semaphore_signal(cred.at[0], inc=1, device_id=dev_c, device_id_type=MESH)
+    cp_mod = remote(modb.at[tp], modb.at[tp], dev_y)
+    cp_mod.start()
+    half = L // 2
+    cp_wo = remote(
+        wo_h.at[pl.ds(al(c * half, 16), half)], wo.at[tp, pl.ds(al(c * half, 16), half)], dev_y
+    )
+    cp_wo.start()
+    ld_wo = load(wo_h, wo.at[tp, 0:L])
+    ld_cot = load(cot_h, cot)
+    ld_w1 = load(w1_h, w1)
+    ld_w2 = load(w2_h, w2)
+    ld_tok.wait()
+    cp_mod.wait()
+
+    def mvec(which, img):
+        return modb[which // 3, img : img + 1, (which % 3) * D : (which % 3 + 1) * D]
+
+    def rows_loop(img, body, init=None, step=RC):
+        base = img * SEQ
+
+        def one(r, carry):
+            return body(pl.ds(al(base + r * step, step), step), carry)
+
+        return lax.fori_loop(0, SEQ // step, one, init)
+
+    def zeros8(n):
+        return tuple(jnp.zeros((8, D), F32) for _ in range(n))
+
+    def total(part):
+        return jnp.sum(part, axis=0, keepdims=True)
+
+    for img in range(2):
+        shift, sc = mvec(0, img), 1.0 + mvec(1, img)
+
+        def body(rows, carry):
+            normed, _ = norm_parts(tok[rows, :].astype(F32))
+            ia[rows, :] = (normed * sc + shift).astype(BF16)
+            return carry
+
+        rows_loop(img, body, 0)
+
+    for j in range(3):
+        ld_w3[j].wait()
+
+    def qkv_body(j, carry):
+        qkv[j] = (dot_nt(ia[...], w3[j]) + qvb_r[j]).astype(BF16)
+        return carry
+
+    lax.fori_loop(0, 3, qkv_body, 0)
+
+    lane = lax.broadcasted_iota(jnp.int32, (1, 256), 1)
+
+    def head_mask(j, e):
+        lo = 16 * j + 72 * e
+        return jnp.where((lane >= lo) & (lane < lo + 72), 1.0, 0.0).astype(BF16)
+
+    def keep_low(j, old, new):
+        full = lax.broadcasted_iota(jnp.int32, new.shape, 1)
+        return jnp.where(full < 16 * j, old.astype(F32), new).astype(BF16)
+
+    def attend(img):
+        rows = slice(img * SEQ, (img + 1) * SEQ)
+
+        def pair(j, carry):
+            win = pl.ds(al(j * 128, 128), 256)
+            q, k, v = qkv[0, rows, win], qkv[1, rows, win], qkv[2, rows, win]
+            mixed = None
+            for e in range(2):
+                mask = head_mask(j, e)
+                s = dot_nt(q * mask, k) * scale
+                p = jnp.exp(s - jnp.max(s, axis=-1, keepdims=True))
+                p = p * (1.0 / jnp.sum(p, axis=-1, keepdims=True))
+                low = p.astype(BF16)
+                prob[img * 8 + 2 * j + e] = low
+                part = dot_nn(low, v * mask)
+                mixed = part if mixed is None else mixed + part
+            merged = keep_low(j, att[tp, rows, win], mixed)
+            att[tp, rows, win] = merged
+            g4[3, rows, win] = merged
+            return carry
+
+        lax.fori_loop(0, 4, pair, 0)
+        cp = remote(att.at[tp, rows], att.at[tp, rows], dev_y)
+        cp.start()
+        return cp
+
+    cp_att = [attend(0)]
+    cp_wo.wait()
+    cp_wf = remote(
+        wo.at[1 - tp, pl.ds(al(c * half, 16), half)],
+        wo.at[1 - tp, pl.ds(al(c * half, 16), half)],
+        dev_c,
+    )
+    cp_wf.start()
+    cp_att.append(attend(1))
+
+    ld_cot.wait()
+    acc = zeros8(1)
+    for img in range(2):
+        gate_b = mvec(5, img)
+
+        def body(rows, carry):
+            low = (cot[rows, :].astype(F32) * gate_b).astype(BF16)
+            gb[rows, :] = low
+            return (carry[0] + fold_rows(low.astype(F32)),)
+
+        acc = rows_loop(img, body, acc)
+    brow_o[1:2, :] = total(acc[0])
+
+    def transpose_to(src, dst, base):
+        def body(t, carry):
+            cols = pl.ds(al(t * 128, 128), 128)
+            dst[cols, base : base + T] = src[:, cols].T
+            return carry
+
+        lax.fori_loop(0, D // 128, body, 0)
+
+    transpose_to(gb, at1, 0)
+
+    ld_wo.wait()
+    cp_wf.wait()
+    ld_w1.wait()
+    ld_w2.wait()
+
+    def feed(img):
+        rows = slice(img * SEQ, (img + 1) * SEQ)
+        cp_att[img].wait()
+
+        def proj(n, carry):
+            cols = pl.ds(al(n * PW, 128), PW)
+            attn[rows, cols] = (
+                dot_nn(att[0, rows, :], wo[0, :, cols])
+                + dot_nn(att[1, rows, :], wo[1, :, cols])
+                + ob_r[:, cols]
+            )
+            return carry
+
+        lax.fori_loop(0, D // PW, proj, 0)
+        gate_a, shift_b, sc_b = mvec(2, img), mvec(3, img), 1.0 + mvec(4, img)
+
+        def body(r, carry):
+            m = tok[r, :].astype(F32) + gate_a * attn[r, :]
+            mid[r, :] = m
+            normed, _ = norm_parts(m)
+            ib[r, :] = (normed * sc_b + shift_b).astype(BF16)
+            return carry
+
+        rows_loop(img, body, 0)
+
+        def hidden(f, carry):
+            cols = pl.ds(al(f * 256, 128), 256)
+            pre = dot_nn(ib[rows, :], w1[:, cols]) + b1_r[:, cols]
+            gh = dot_nt(gb[rows, :], w2[cols, :])
+            sq = pre * pre
+            th = jnp.tanh(GELU_COEF * pre * (1.0 + GELU_CUBE * sq))
+            hp = 0.5 + 0.5 * th
+            hid[rows, cols] = (pre * hp).astype(BF16)
+            slope = hp + (0.5 * GELU_COEF) * pre * (1.0 - th * th) * (
+                1.0 + (3.0 * GELU_CUBE) * sq
+            )
+            low = (gh * slope).astype(BF16)
+            gpre[rows, cols] = low
+            col_sum = jnp.sum(low.astype(F32), axis=0, keepdims=True)
+            if img == 0:
+                bfc1_o[:, cols] = col_sum
+            else:
+                bfc1_o[:, cols] = bfc1_o[:, cols] + col_sum
+            return carry
+
+        lax.fori_loop(0, F // 256, hidden, 0)
+
+        def back(n, carry):
+            cols = pl.ds(al(n * PW, 128), PW)
+            gibs[rows, cols] = dot_nt(gpre[rows, :], w1[cols, :]).astype(BF16)
+            return carry
+
+        lax.fori_loop(0, D // PW, back, 0)
+        cp = remote(gibs.at[rows], gibr.at[rows], dev_y)
+        cp.start()
+        return cp
+
+    cp_gib = [feed(0), feed(1)]
+
+
+    LO1, LO2 = 2 * LP, 2 * LP + T
+    pl.semaphore_signal(cred.at[1], inc=1, device_id=dev_c, device_id_type=MESH)
+    pl.semaphore_wait(cred.at[0], 1)
+    cp_c, cp_x, cp_z, cp_w, cp_f, cp_o = {}, {}, {}, {}, {}, {}
+
+    def place(s):
+        zz, xx = s // 2, s % 2
+        return (xx * 4 + (zz % 2) * 2 + zz // 2) * blk
+
+    def product(p, h):
+        if p < 2 * NP:
+            cols = pl.ds(al(h * (F // 2) + PW * (p % NP), 128), PW)
+            return dot_nn(at1[...], (hid if p < NP else gpre)[:, cols])
+        q = p - 2 * NP
+        base = LO1 if q == 0 else al(LO1 + h * T, 128)
+        return dot_nn(w1[:, pl.ds(base, T)], g4[2 * h + q])
+
+    def land_c(p):
+        if p < 2 * NP:
+            return big.at[p]
+        return w1.at[:, (p - 2 * NP) * LP : (p - 2 * NP + 1) * LP]
+
+    def land(plain, wide, p):
+        return plain.at[p] if p < 2 * NP else wide.at[p - 2 * NP]
+
+    def theirs(p):
+        res = product(p, 1 - c)
+        if p < 2 * NP:
+            slot = big.at[6 + p % NP]
+            if p >= NP:
+                cp_c[p - NP].wait_send()
+        else:
+            slot = w2.at[0:D, 0:LP]
+            if p == 2 * NP:
+                pl.semaphore_wait(cred.at[1], 1)
+            else:
+                cp_c[p - 1].wait_send()
+        for s in range(8):
+            slot[place(s) : place(s) + blk, :] = res[s * blk : (s + 1) * blk].astype(BF16)
+        cp_c[p] = remote(slot, land_c(p), dev_c)
+        cp_c[p].start()
+
+    def mine(p):
+        res = product(p, c)
+        cp_c[p].wait_recv()
+        ref = land_c(p)
+        for s in range(8):
+            rows = slice(place(s), place(s) + blk)
+            ref[rows, :] = (res[s * blk : (s + 1) * blk] + ref[rows, :].astype(F32)).astype(BF16)
+        rows = pl.ds(al((1 - x) * 4 * blk, 16), 4 * blk)
+        cp_x[p] = remote(ref.at[rows], land(rx, rx3, p), dev_x)
+        cp_x[p].start()
+
+    def merge(p, base, arrived, count):
+        ref = land_c(p)
+
+        def body(i, carry):
+            rows = pl.ds(al(base + i * blk, 16), blk)
+            got = arrived[pl.ds(al(i * blk, 16), blk), :].astype(F32)
+            ref[rows, :] = (ref[rows, :].astype(F32) + got).astype(BF16)
+            return carry
+
+        lax.fori_loop(0, count, body, 0)
+
+    base_x = x * 4 * blk
+    base_z = base_x + zp * 2 * blk
+    base_w = base_z + zh * blk
+
+    def step_x(p):
+        cp_x[p].wait_recv()
+        merge(p, base_x, land(rx, rx3, p), 4)
+        rows = pl.ds(al(base_x + (1 - zp) * 2 * blk, 16), 2 * blk)
+        cp_z[p] = remote(land_c(p).at[rows], land(rz, rz3, p), dev_z)
+        cp_z[p].start()
+
+    def step_z(p):
+        cp_z[p].wait_recv()
+        merge(p, base_z, land(rz, rz3, p), 2)
+        rows = pl.ds(al(base_z + (1 - zh) * blk, 16), blk)
+        cp_w[p] = remote(land_c(p).at[rows], land(ry, ry3, p), dev_w)
+        cp_w[p].start()
+
+    def drain(p):
+        cp_o[p].wait()
+        cp_f[p].wait_send()
+
+    def step_w(p):
+        cp_w[p].wait_recv()
+        both = land_c(p)[pl.ds(al(base_w, 16), blk), :].astype(F32)
+        both = (both + land(ry, ry3, p)[...].astype(F32)) * factor
+        keep, give = pl.ds(al(c * (blk // 2), 8), blk // 2), pl.ds(al((1 - c) * (blk // 2), 8), blk // 2)
+        if p < 2 * NP:
+            if p >= 2:
+                drain(p - 2)
+            stage = fin.at[p % 2]
+            stage[...] = both
+            cols = pl.ds(al(c * (F // 2) + PW * (p % NP), 128), PW)
+            dst = (g2_h if p < NP else g1_h).at[:, cols]
+        else:
+            stage = fin3.at[p - 2 * NP]
+            stage[...] = both[:, 0:L]
+            dst = g3_h.at[2 * c + p - 2 * NP]
+        cp_o[p] = store(stage.at[keep], dst)
+        cp_f[p] = remote(stage.at[give], dst, dev_c)
+        cp_f[p].start()
+
+    def branch(img):
+        rows = slice(img * SEQ, (img + 1) * SEQ)
+
+        def body(n, carry):
+            cols = pl.ds(al(n * PW, 128), PW)
+            ib[rows, cols] = dot_nn(hid[rows, :], w2[:, cols]).astype(BF16)
+            return carry
+
+        lax.fori_loop(0, D // PW, body, 0)
+
+    def send_branch():
+        pl.semaphore_signal(cred.at[4], inc=1, device_id=dev_y, device_id_type=MESH)
+        pl.semaphore_wait(cred.at[4], 1)
+        cp = remote(ib, w2.at[D : D + T], dev_y)
+        cp.start()
+        return cp
+
+    bo_acc = [zeros8(1)[0]]
+    tails = []
+
+    def norm_b_back(img):
+        cp_gib[img].wait()
+        gate_a, sc_b = mvec(2, img), 1.0 + mvec(4, img)
+
+        def body(r, carry):
+            s_shift, s_scale, s_gate, s_bias = carry
+            g = gibs[r, :].astype(F32) + gibr[r, :].astype(F32)
+            normed, inv = norm_parts(mid[r, :])
+            s_shift += fold_rows(g)
+            s_scale += fold_rows(g * normed)
+            u = g * sc_b
+            m1 = jnp.mean(u, axis=-1, keepdims=True)
+            m2 = jnp.mean(u * normed, axis=-1, keepdims=True)
+            gm = cot[r, :].astype(F32) + inv * (u - m1 - normed * m2)
+            s_gate += fold_rows(gm * attn[r, :])
+            low = (gm * gate_a).astype(BF16)
+            gb[r, :] = low
+            s_bias += fold_rows(low.astype(F32))
+            attn[r, :] = gm
+            return (s_shift, s_scale, s_gate, s_bias)
+
+        sums = rows_loop(img, body, zeros8(3) + (bo_acc[0],))
+        pl.semaphore_signal(cred.at[2 + img], inc=1, device_id=dev_y, device_id_type=MESH)
+        gmod[1, img : img + 1, 0:D] = total(sums[0])
+        gmod[1, img : img + 1, D : 2 * D] = total(sums[1])
+        gmod[0, img : img + 1, 2 * D : 3 * D] = total(sums[2])
+        bo_acc[0] = sums[3]
+        if img == 1:
+            brow_o[0:1, :] = total(bo_acc[0])
+
+    def attend_back(img):
+        rows = slice(img * SEQ, (img + 1) * SEQ)
+        att[1 - tp, rows, :] = dot_nt(gb[rows, :], wo[tp]).astype(BF16)
+
+        def pair(j, carry):
+            win = pl.ds(al(j * 128, 128), 256)
+            q, k, v = qkv[0, rows, win], qkv[1, rows, win], qkv[2, rows, win]
+            g = att[1 - tp, rows, win]
+            gq = gk = gv = None
+            for e in range(2):
+                mask = head_mask(j, e)
+                gm = g * mask
+                low = prob[img * 8 + 2 * j + e]
+                p = low.astype(F32)
+                gp = dot_nt(gm, v)
+                ds = (p * (gp - jnp.sum(p * gp, axis=-1, keepdims=True))).astype(BF16)
+                parts = dot_nn(ds, k * mask), dot_tn(ds, q * mask), dot_tn(low, gm)
+                if gq is None:
+                    gq, gk, gv = parts
+                else:
+                    gq, gk, gv = gq + parts[0], gk + parts[1], gv + parts[2]
+            g4[0, rows, win] = keep_low(j, g4[0, rows, win], gq * scale)
+            g4[1, rows, win] = keep_low(j, g4[1, rows, win], gk * scale)
+            g4[2, rows, win] = keep_low(j, g4[2, rows, win], gv)
+            return carry
+
+        lax.fori_loop(0, 4, pair, 0)
+        for n, which in enumerate((0, 2)):
+            cur = jnp.sum(g4[which, rows, :].astype(F32), axis=0, keepdims=True)
+            bqv_o[n : n + 1, :] = cur if img == 0 else bqv_o[n : n + 1, :] + cur
+
+        def body(n, carry):
+            cols = pl.ds(al(n * PW, 128), PW)
+            part = dot_nn(g4[0, rows, :], w3[0, :, cols])
+            part += dot_nn(g4[1, rows, :], w3[1, :, cols])
+            part += dot_nn(g4[2, rows, :], w3[2, :, cols])
+            gibs[rows, cols] = part.astype(BF16)
+            return carry
+
+        lax.fori_loop(0, D // PW, body, 0)
+        pl.semaphore_wait(cred.at[2 + img], 1)
+        cp = remote(gibs.at[rows], gibr.at[rows], dev_y)
+        cp.start()
+        return cp
+
+    def norm_a_back(img, cp):
+        cp.wait()
+        sc_a = 1.0 + mvec(1, img)
+
+        def body(r, carry):
+            s_shift, s_scale = carry
+            g = gibs[r, :].astype(F32) + gibr[r, :].astype(F32)
+            normed, inv = norm_parts(tok[r, :].astype(F32))
+            s_shift += fold_rows(g)
+            s_scale += fold_rows(g * normed)
+            u = g * sc_a
+            m1 = jnp.mean(u, axis=-1, keepdims=True)
+            m2 = jnp.mean(u * normed, axis=-1, keepdims=True)
+            gb[r, :] = (attn[r, :] + inv * (u - m1 - normed * m2)).astype(BF16)
+            return (s_shift, s_scale)
+
+        sums = rows_loop(img, body, zeros8(2))
+        gmod[0, img : img + 1, 0:D] = total(sums[0])
+        gmod[0, img : img + 1, D : 2 * D] = total(sums[1])
+        rows = slice(img * SEQ, (img + 1) * SEQ)
+        tails.append(store(gb.at[rows], gt_h.at[rows]))
+
+    def finish(img):
+        gate_b = mvec(5, img)
+
+        def body(r, carry):
+            br = ib[r, :].astype(F32) + w2[pl.ds(al(D + r.start, RC), RC), :].astype(F32) + b2_r[...]
+            ia[r, :] = (mid[r, :] + gate_b * br).astype(BF16)
+            return (carry[0] + fold_rows(cot[r, :].astype(F32) * br),)
+
+        sums = rows_loop(img, body, zeros8(1))
+        gmod[1, img : img + 1, 2 * D : 3 * D] = total(sums[0])
+        rows = slice(img * SEQ, (img + 1) * SEQ)
+        tails.append(store(ia.at[rows], out_h.at[rows]))
+
+    theirs(0)
+    theirs(1)
+    mine(0)
+    theirs(2)
+    mine(1)
+    mine(2)
+    transpose_to(ib, at1, 0)
+    transpose_to(ia, w1, LO1)
+    norm_b_back(0)
+    cp_gia = [attend_back(0)]
+    branch(0)
+    branch(1)
+    step_x(0)
+    theirs(3)
+    theirs(4)
+    mine(3)
+    norm_b_back(1)
+    transpose_to(gb, w1, LO2)
+    cp_gia.append(attend_back(1))
+    cp_br = send_branch()
+    step_x(1)
+    step_z(0)
+    mine(4)
+    theirs(5)
+    mine(5)
+    theirs(6)
+    mine(6)
+    theirs(7)
+    mine(7)
+    step_w(0)
+    step_x(2)
+    step_z(1)
+    step_w(1)
+    step_x(3)
+    step_z(2)
+    step_w(2)
+    norm_a_back(0, cp_gia[0])
+    norm_a_back(1, cp_gia[1])
+    step_x(4)
+    step_z(3)
+    step_w(3)
+    cp_br.wait()
+    finish(0)
+    finish(1)
+    gmod_o[...] = gmod[tp]
+    step_x(5)
+    step_z(4)
+    step_w(4)
+    step_x(6)
+    step_z(5)
+    step_w(5)
+    step_x(7)
+    step_z(6)
+    step_w(6)
+    step_z(7)
+    step_w(7)
+
+    for p in range(2 * NP + 2):
+        if p >= NP and p != 2 * NP:
+            cp_c[p].wait_send()
+        cp_x[p].wait_send()
+        cp_z[p].wait_send()
+        cp_w[p].wait_send()
+        if p >= 2 * NP - 2:
+            drain(p)
+        cp_f[p].wait_recv()
+    for cp in tails:
+        cp.wait()
+
+
+def fused(
+    tokens, condition, noise_times, cotangent, ada_weight, ada_bias, qkv_weight, qv_bias,
+    out_weight, out_bias, fc1_weight, fc1_bias, fc2_weight, fc2_bias,
+):
+    T, width = tokens.shape
+    L, F, A = qkv_weight.shape[2], fc1_weight.shape[1], ada_weight.shape[1]
+    LP = -(-L // 128) * 128
+    n_dp = lax.axis_size("dp")
+    blk = width // 8
+    factor = 1.0 / math.sqrt(T * n_dp)
+    cond_total = condition + time_features(noise_times)
+    silu_cond, silu_pull = jax.vjp(jax.nn.silu, cond_total)
+    silu_low = silu_cond.astype(BF16)
+    silu_rows = jnp.pad(silu_low.astype(F32), ((0, 6), (0, 0)))
+    pad = ((0, 0), (0, LP - L))
+    qvb = jnp.pad(qv_bias, pad)
+    qvb = jnp.stack([qvb[0:1], jnp.zeros((1, LP), F32), qvb[1:2]])
+    w3 = jnp.transpose(qkv_weight, (1, 2, 0))
+    hbm, vmem = pl.BlockSpec(memory_space=pl.ANY), pl.BlockSpec(memory_space=pltpu.VMEM)
+    sds = jax.ShapeDtypeStruct
+    results = pl.pallas_call(
+        functools.partial(block_kernel, factor),
+        out_shape=(
+            sds((T, width), BF16), sds((T, width), BF16),
+            sds((width // n_dp, F), F32), sds((width // n_dp, F), F32),
+            sds((4, width // n_dp, L), F32),
+            sds((2, A), F32), sds((1, F), F32), sds((2, width), F32), sds((2, LP), F32),
+        ),
+        in_specs=[hbm] * 7 + [vmem] * 6,
+        out_specs=(hbm,) * 5 + (vmem,) * 4,
+        scratch_shapes=[
+            pltpu.VMEM((A // PW, width, PW), BF16),
+            pltpu.VMEM((3, LP, width), BF16),
+            pltpu.VMEM((2, LP, width), BF16),
+            pltpu.VMEM((width, F), BF16),
+            pltpu.VMEM((F, width), BF16),
+            pltpu.VMEM((T, width), BF16),
+            pltpu.VMEM((T, width), BF16),
+            pltpu.VMEM((T, width), BF16),
+            pltpu.VMEM((T, width), BF16),
+            pltpu.VMEM((T, width), BF16),
+            pltpu.VMEM((3, T, LP), BF16),
+            pltpu.VMEM((16, T // 2, T // 2), BF16),
+            pltpu.VMEM((2, T, LP), BF16),
+            pltpu.VMEM((T, width), F32),
+            pltpu.VMEM((T, width), F32),
+            pltpu.VMEM((T, F), BF16),
+            pltpu.VMEM((T, F), BF16),
+            pltpu.VMEM((T, width), BF16),
+            pltpu.VMEM((T, width), BF16),
+            pltpu.VMEM((4, T, LP), BF16),
+            pltpu.VMEM((width, T), BF16),
+            pltpu.VMEM((6, 4 * blk, PW), BF16),
+            pltpu.VMEM((2, 4 * blk, LP), BF16),
+            pltpu.VMEM((6, 2 * blk, PW), BF16),
+            pltpu.VMEM((2, 2 * blk, LP), BF16),
+            pltpu.VMEM((6, blk, PW), BF16),
+            pltpu.VMEM((2, blk, LP), BF16),
+            pltpu.VMEM((2, blk, PW), F32),
+            pltpu.VMEM((2, blk, L), F32),
+            pltpu.VMEM((2, 2, A), F32),
+            pltpu.VMEM((2, 2, A), F32),
+            pltpu.SemaphoreType.DMA((24,)),
+            pltpu.SemaphoreType.DMA((16,)),
+            pltpu.SemaphoreType.DMA((64,)),
+            pltpu.SemaphoreType.DMA((64,)),
+            pltpu.SemaphoreType.REGULAR((8,)),
+        ],
+        compiler_params=pltpu.CompilerParams(
+            collective_id=0, has_side_effects=True, vmem_limit_bytes=63 * 2**20
+        ),
+        name="block",
+    )(
+        tokens, cotangent, ada_weight, w3, out_weight, fc1_weight, fc2_weight,
+        silu_rows, ada_bias[None], qvb, out_bias[None], fc1_bias[None], fc2_bias[None],
+    )
+    output, grad_tokens, g2, g1, g4, grad_mod, b_fc1, b_row, b_qv = results
+    sizes = jnp.concatenate([b_fc1[0], b_row.reshape(-1), b_qv.reshape(-1)])
+    mine = jnp.concatenate([grad_mod.reshape(-1), silu_low.astype(F32).reshape(-1), sizes])
+    every = lax.all_gather(mine, "dp", axis=0)
+    mod_all = every[:, : 2 * A].reshape(2 * n_dp, A)
+    silu_all = every[:, 2 * A : 2 * A + 2 * width].reshape(2 * n_dp, width)
+    sums = jnp.sum(every[:, 2 * A + 2 * width :], axis=0) * factor
+    rows = width // n_dp
+    silu_cols = lax.dynamic_slice_in_dim(silu_all, lax.axis_index("dp") * rows, rows, 1)
+    grad_ada = (
+        lax.dot_general(
+            silu_cols, mod_all, (((0,), (0,)), ((), ())),
+            precision=lax.Precision.HIGHEST, preferred_element_type=F32,
+        )
+        * factor
+    )
+    ada_sum = jnp.sum(mod_all, axis=0) * factor
+    silu_part = lax.dot_general(
+        grad_mod, ada_weight.astype(F32), (((1,), (1,)), ((), ())),
+        precision=lax.Precision.HIGHEST, preferred_element_type=F32,
+    )
+    grad_condition = silu_pull(lax.psum(silu_part, "tp"))[0]
+    s_fc1, s_row, s_qv = sums[:F], sums[F : F + 2 * width].reshape(2, width), sums[F + 2 * width :].reshape(2, LP)
+    return (
+        output, grad_tokens, grad_condition, grad_ada, ada_sum,
+        jnp.transpose(g4[0:3], (1, 0, 2)), s_qv[:, :L],
+        g4[3].T, s_row[0], g1, s_fc1, g2.T, s_row[1],
+    )
+
+
+def local(*args):
+    tokens, condition, qkv_weight, fc1_weight = args[0], args[1], args[6], args[10]
+    fits = (
+        lax.axis_size("tp") == 2 and lax.axis_size("dp") == 16
+        and condition.shape[0] == 2 and tokens.shape[0] == 2 * SEQ
+        and qkv_weight.shape[2] == D // 2 and fc1_weight.shape[1] == 2 * D
+    )
+    return fused(*args) if fits else plain(*args)
 
 
 def solution(mesh):

time: 764 us -> 249 us (0.33)
  waiting for transfers between devices: 483 us -> 0 us
  Pallas kernels: 0 us -> 188 us
  matrix products: 94.9 us -> 11.6 us
  blocking collectives: 69.8 us -> 27.9 us
  other arithmetic: 45.4 us -> 3.72 us
  local copies, waits for them, and re-layouts: 47 us -> 16.1 us
  between operations: 14.7 us -> 0.88 us
    unnamed x12 -> x0, waiting for transfers between devices: 223 us -> none
    pallas_call x0 -> x1, Pallas kernels: none -> 188 us  [fused(): pl.pallas_call(functools.partial(block_kernel, factor), out_shape=(sds((T...]
    psum x4 -> x0, waiting for transfers between devices: 182 us -> none  [the longest x1 67.7 us: local(): attention = lax.psum(attn_part, 'tp') + out_bias]
    dot_general x21 -> x2, matrix products: 94.9 us -> 11.6 us  [the longest x1 9.61 us: fused(): lax.dot_general(grad_mod, ada_weight.astype(F32), (((1,), (1,)), ((), ())...]
    reduce_scatter x2 -> x0, waiting for transfers between devices: 78.2 us -> none  [the longest x1 78.2 us: local(): lax.psum_scatter(weight_fc1.astype(jnp.bfloat16), 'dp', scatter_dimension...]
    psum x2 -> x1, blocking collectives: 64.4 us -> 5.06 us  [fused(): grad_condition = silu_pull(lax.psum(silu_part, 'tp'))[0]]
    unnamed x78 -> x26, local copies, waits for them, and re-layouts: 42 us -> 5.23 us
    reduce_sum x13 -> x2, other arithmetic: 27.7 us -> 0.1 us  [the longest x1 0.06 us: fused(): sums = jnp.sum(every[:, 2 * A + 2 * width:], axis=0) * factor]
  transfers between devices with their start and end apart: 9 -> 0, of which waited for: 8 -> 0; matrix products, arithmetic and copies ran while one was open for 15% -> 0% of each run, Pallas kernels for 0% -> 0%
where the time goes in v1:
time: 249 us; the launch traced here: 248 us
  Pallas kernels  188 us (76%)
  blocking collectives  27.9 us (11%)
  local copies, waits for them, and re-layouts  16.1 us (6%)
  matrix products  11.6 us (5%)
  other arithmetic  3.72 us (1%)
    pallas_call x1, Pallas kernels, fused(): pl.pallas_call(functools.partial(block_kernel, factor), out_shape=(sds((T...  188 us
    all_gather x1, blocking collectives, fused(): every = lax.all_gather(mine, 'dp', axis=0)  22.8 us
    dot_general x1, matrix products, fused(): lax.dot_general(grad_mod, ada_weight.astype(F32), (((1,), (1,)), ((), ())...  9.61 us
    unnamed x26, local copies, waits for them, and re-layouts  5.23 us
    psum x1, blocking collectives, fused(): grad_condition = silu_pull(lax.psum(silu_part, 'tp'))[0]  5.06 us

profile of v1, /device:TPU:0, one launch (start us, length us, event | category | flops | bytes accessed | tf_op | source)
XLA Modules:
  0.0 248.4 jit_solution(431011375889413687)
XLA Ops:
  0.6 0.7 broadcast_multiply_fusion.2
  1.3 0.1 pad.11.clone
  1.4 1.3 broadcast_in_dim.15.ob_r
  2.7 1.3 broadcast_in_dim.17.b2_r
  4.0 0.8 fusion.4
  4.8 0.7 pad_maximum_fusion.qvb_r
  5.4 0.2 multiply_cosine_fusion
  5.6 0.8 fusion.3
  6.4 1.3 broadcast_in_dim.16.b1_r
  7.7 1.3 broadcast_in_dim.14.adab_r
  9.0 0.6 pad.8.silu_r
  9.6 188.1 %block.1 = (bf16[512,1152]{1,0:T(8,128)(2,1)}, bf16[512,1152]{1,0:T(8,128)(2,1)}, f32[72,2304]{1,0:T(8,128)}, f32[72,2304]{1,0:T(8,128)}, f32[4,72,576]{2,1,0:T(...) custom-call(bf16[512,1152]{1,0:T(8,128)(2,1)} %tok_h.1, ...), custom_call_target="tpu_custom_call" | custom-call | tf_op jit(solution)/shard_map/block/pallas_call | solution.py:882
  197.8 0.7 reshape.63
  198.5 0.0 copy-start.5
  198.5 0.0 copy-start.4
  198.5 0.0 copy-start.7
  198.5 0.0 copy-start.6
  198.5 0.0 copy-start.1
  198.5 9.6 %fusion.8 = f32[2,1152]{1,0:T(2,128)S(1)} fusion(f32[2,3456]{1,0:T(2,128)} %get-tuple-element.24, bf16[1152,3456]{1,0:T(8,128)(2,1)} %ada_h.1), kind=kOutput, calls=%fused_computation.31 | convolution fusion | flops 95551488 | bytes 7999488 | tf_op jit(solution)/shard_map/dot_general | solution.py:955
  208.1 5.1 %psum.7 = f32[2,1152]{1,0:T(2,128)S(1)} all-reduce(f32[2,1152]{1,0:T(2,128)S(1)} %fusion.8), channel_id=1, replica_groups=mesh['dp'=16,'tp'=2] {'tp'}, use_global_device_ids=true, to_apply=%region_0.1 | all-reduce | flops 2304 | bytes 18432 | tf_op jit(solution)/shard_map/psum | solution.py:959
  213.2 0.0 copy-done.5
  213.2 0.7 fusion.2
  213.9 0.0 copy-done.4
  214.0 0.0 copy-done.7
  214.0 0.0 copy-done.6
  214.1 0.0 copy-done.1
  214.1 0.7 slice_bitcast_fusion.1
  214.8 0.8 slice_bitcast_fusion
  215.7 22.8 %all-gather.1 = f32[16,1,15104]{2,1,0:T(1,128)S(1)} all-gather(f32[1,1,15104]{2,1,0:T(1,128)S(1)} %reshape.68), channel_id=2, replica_groups=mesh['dp'=16,'tp'=2] {'dp'}, dimensions={0}, use_global_device_ids=true | all-gather | bytes 1027072 | tf_op jit(solution)/shard_map/all_gather | solution.py:941
  238.5 0.1 copy.29
  238.5 0.0 copy-start
  238.6 0.1 slice_reduce_fusion
  238.6 0.6 reshape.66
  239.2 0.6 slice.59
  239.8 0.6 fusion.7
  240.5 0.0 copy-start.3
  240.5 0.1 reshape.65
  240.6 0.0 copy-start.2
  240.7 0.6 broadcast_multiply_fusion.1
  241.3 2.0 convolution_multiply_fusion
  243.3 2.4 copy.39
  245.7 0.0 copy-done
  245.7 1.0 copy.40
  246.7 0.0 copy-done.3
  246.7 0.8 copy.41
  247.5 0.0 copy-done.2
  247.6 0.8 copy.42
  (18 shorter events, 0.3 us)
Async XLA Ops:
  198.5 14.7 %copy-start.5 = (f32[2,1152]{1,0:T(2,128)S(1)}, f32[2,1152]{1,0:T(2,128)}, u32[]{:S(2)}) copy-start(f32[2,1152]{1,0:T(2,128)} %param.15) | copy-start | bytes 27652
  198.5 15.4 %copy-start.4 = (f32[2,3456]{1,0:T(2,128)S(1)}, f32[2,3456]{1,0:T(2,128)}, u32[]{:S(2)}) copy-start(f32[2,3456]{1,0:T(2,128)} %get-tuple-element.24) | copy-start | bytes 82948
  198.5 15.5 %copy-start.7 = (f32[1,2304]{1,0:T(1,128)S(1)}, f32[1,2304]{1,0:T(1,128)}, u32[]{:S(2)}) copy-start(f32[1,2304]{1,0:T(1,128)} %get-tuple-element.25) | copy-start | bytes 27652
  198.5 15.5 %copy-start.6 = (f32[2,1152]{1,0:T(2,128)S(1)}, f32[2,1152]{1,0:T(2,128)}, u32[]{:S(2)}) copy-start(f32[2,1152]{1,0:T(2,128)} %get-tuple-element.26) | copy-start | bytes 27652
  198.5 15.6 %copy-start.1 = (f32[4,72,576]{2,1,0:T(8,128)S(1)}, f32[4,72,576]{2,1,0:T(8,128)}, u32[]{:S(2)}) copy-start(f32[4,72,576]{2,1,0:T(8,128)} %get-tuple-element.28) | copy-start | bytes 1990660
  238.5 7.1 %copy-start = (bf16[512,1152]{1,0:T(8,128)(2,1)S(1)}, bf16[512,1152]{1,0:T(8,128)(2,1)}, u32[]{:S(2)}) copy-start(bf16[512,1152]{1,0:T(8,128)(2,1)} %get-tuple-element.51) | copy-start | bytes 3538948
  240.5 6.2 %copy-start.3 = (f32[72,2304]{1,0:T(8,128)S(1)}, f32[72,2304]{1,0:T(8,128)}, u32[]{:S(2)}) copy-start(f32[72,2304]{1,0:T(8,128)} %get-tuple-element.59) | copy-start | bytes 1990660
  240.6 6.9 %copy-start.2 = (f32[72,2304]{1,0:T(8,128)S(1)}, f32[72,2304]{1,0:T(8,128)}, u32[]{:S(2)}) copy-start(f32[72,2304]{1,0:T(8,128)} %get-tuple-element.30) | copy-start | bytes 1990660
